TPU v7x, 32 devices: a whole 2x2x4 slice. The times are simulated.
32 devices in a mesh: ctx: 8 (over z, y), head: 4 (over x, core).
Axes of the slice: x: 2, y: 2, z: 4, core: 2. Of those that a mesh axis runs over, the one named last changes fastest.
Arguments:
- query: bfloat16 [4096, 4096], P(('ctx', 'head')), may hold values from -16 to 16
- key: bfloat16 [4096, 4096], P(('ctx', 'head')), may hold values from -4.5 to 4.5
- value: bfloat16 [4096, 4096], P(('ctx', 'head')), may hold values from -12 to 12
- out_grad: bfloat16 [4096, 4096], P(('ctx', 'head')), may hold values from -6 to 6
- offsets: int32 [2, 32], P(None, 'head'), may hold values from 0 to 63, as said below
Outputs:
- attended: bfloat16 [4096, 4096], P(('ctx', 'head'))
- query_grad: bfloat16 [4096, 4096], P(('ctx', 'head'))
- key_grad: bfloat16 [4096, 4096], P(('ctx', 'head'))
- value_grad: bfloat16 [4096, 4096], P(('ctx', 'head'))
Inputs may be any that keep to these rules, and one draw needn't show every extreme that they name: `offsets`: row 0 holds values 0 to 15 with 15 among them; row 1 holds values 0 to 63 with 63 among them.
All inputs are finite; a program needn't handle non-finite values.
Results may differ from a plain program's by a relative error of at most 0.04.
Values may be sent and summed in bfloat16 or wider, within the bound.
A program may use at most 128 MiB of HBM per device.

v0:
```python
import jax
import jax.numpy as jnp
from jax import lax
from jax.sharding import PartitionSpec as P

MIDDLE_DILATION = 16
UPPER_DILATION = 64


def partner(block, axis, bit):
    count = lax.axis_size(axis)
    route = []
    for low in range(count):
        high = low | 1 << bit
        if high != low and high < count:
            route += [(low, high), (high, low)]
    return lax.ppermute(block, axis, route)


def head_mask(dilation_rate, start_offset, ndim):
    heads = start_offset.shape[0]
    mask = lax.broadcasted_iota(jnp.int32, (dilation_rate, heads), 0) == start_offset[None, :]
    return mask.reshape((1, dilation_rate, heads) + (1,) * (ndim - 2))


def selector(values, dilation_rate, start_offset):
    if dilation_rate == 1:
        return values
    shaped = values.reshape((values.shape[0] // dilation_rate, dilation_rate) + values.shape[1:])
    mask = head_mask(dilation_rate, start_offset, values.ndim)
    return jnp.sum(jnp.where(mask, shaped, jnp.zeros((), values.dtype)), axis=1)


def spread_factor(rows, dilation_rate, start_offset):
    if dilation_rate == 1:
        return rows
    mask = head_mask(dilation_rate, start_offset, rows.ndim)
    full = jnp.where(mask, rows[:, None], jnp.zeros((), rows.dtype))
    return full.reshape((rows.shape[0] * dilation_rate,) + rows.shape[1:])


def merge_top(current, rows, dilation_rate, start_offset):
    shaped = current.reshape((current.shape[0] // dilation_rate, dilation_rate) + current.shape[1:])
    mask = head_mask(dilation_rate, start_offset, current.ndim)
    shaped = jnp.where(mask, jnp.maximum(shaped, rows[:, None]), shaped)
    return shaped.reshape(current.shape)


def doubled(piece, bits, trade, place_index):
    for bit in range(bits):
        other = trade(piece, bit)
        upper = place_index // (1 << bit) % 2 == 1
        piece = jnp.where(
            upper, jnp.concatenate([other, piece], 1), jnp.concatenate([piece, other], 1)
        )
    return piece


def halved(total, bits, trade, place_index):
    for bit in reversed(range(bits)):
        half = total.shape[0] // 2
        lower, higher = (total[:half], total[half:])
        upper = place_index // (1 << bit) % 2 == 1
        keep = jnp.where(upper, higher, lower)
        sent = jnp.where(upper, lower, higher)
        total = keep + trade(sent, bit)
    return total


def local(query, key, value, out_grad, offsets):
    heads_dev = offsets.shape[1]
    query, key, value, out_grad = (
        lax.all_to_all(query, "head", split_axis=1, concat_axis=0, tiled=True),
        lax.all_to_all(key, "head", split_axis=1, concat_axis=0, tiled=True),
        lax.all_to_all(value, "head", split_axis=1, concat_axis=0, tiled=True),
        lax.all_to_all(out_grad, "head", split_axis=1, concat_axis=0, tiled=True),
    )
    tok = query.shape[0]
    head_dim = query.shape[1] // heads_dev
    softmax_scale = head_dim ** (-0.5)
    query_full = query.reshape(tok, heads_dev, head_dim)
    key_full = key.reshape(tok, heads_dev, head_dim)
    value_full = value.reshape(tok, heads_dev, head_dim)
    gradient_full = out_grad.reshape(tok, heads_dev, head_dim)
    ctx_count = lax.axis_size("ctx")
    place_index = lax.axis_index("ctx")
    mid_bits = (ctx_count // 4).bit_length() - 1
    middle_offset = offsets[0]
    upper_offset = offsets[1]
    middle_query = selector(query_full, MIDDLE_DILATION, middle_offset)
    middle_gradient = selector(gradient_full, MIDDLE_DILATION, middle_offset)
    middle_owned_rows = jnp.stack(
        [
            selector(key_full, MIDDLE_DILATION, middle_offset),
            selector(value_full, MIDDLE_DILATION, middle_offset),
        ]
    )
    middle_key_rows = doubled(
        middle_owned_rows, mid_bits, lambda piece, bit: partner(piece, "ctx", bit), place_index
    )
    upper_query = selector(query_full, UPPER_DILATION, upper_offset)
    upper_gradient = selector(gradient_full, UPPER_DILATION, upper_offset)
    upper_owned_rows = jnp.stack(
        [
            selector(key_full, UPPER_DILATION, upper_offset),
            selector(value_full, UPPER_DILATION, upper_offset),
        ]
    )
    upper_key_rows = lax.all_gather(upper_owned_rows, "ctx", axis=1, tiled=True)
    levels = [
        (query_full, gradient_full, key_full, value_full, 1, middle_offset),
        (
            middle_query,
            middle_gradient,
            middle_key_rows[0],
            middle_key_rows[1],
            MIDDLE_DILATION,
            middle_offset,
        ),
        (
            upper_query,
            upper_gradient,
            upper_key_rows[0],
            upper_key_rows[1],
            UPPER_DILATION,
            upper_offset,
        ),
    ]
    scores = [
        jnp.einsum("qhd,khd->hqk", lq, lk, preferred_element_type=jnp.float32) * softmax_scale
        for lq, lg, lk, lv, dilation_rate, off in levels
    ]
    top_stat = scores[0].max(-1).T
    for index in (1, 2):
        dilation_rate, off = (levels[index][4], levels[index][5])
        top_stat = merge_top(top_stat, scores[index].max(-1).T, dilation_rate, off)
    total = jnp.zeros((tok, heads_dev), jnp.float32)
    numer = jnp.zeros((tok, heads_dev, head_dim), jnp.float32)
    for index in range(3):
        lq, lg, lk, lv, dilation_rate, off = levels[index]
        shift = selector(top_stat, dilation_rate, off)
        level_weight = jnp.exp(scores[index] - shift.T[:, :, None])
        total = total + spread_factor(level_weight.sum(-1).T, dilation_rate, off)
        part = jnp.einsum(
            "hqk,khd->qhd",
            level_weight.astype(jnp.bfloat16),
            lv,
            preferred_element_type=jnp.float32,
        )
        numer = numer + spread_factor(part, dilation_rate, off)
    attended = (numer / total[:, :, None]).astype(jnp.bfloat16)
    lse = top_stat + jnp.log(total)
    delta = jnp.sum(gradient_full.astype(jnp.float32) * attended.astype(jnp.float32), -1)
    query_grad = jnp.zeros((tok, heads_dev, head_dim), jnp.float32)
    grads_back = []
    for index in range(3):
        lq, lg, lk, lv, dilation_rate, off = levels[index]
        lse_rows = selector(lse, dilation_rate, off)
        delta_rows = selector(delta, dilation_rate, off)
        probability = jnp.exp(scores[index] - lse_rows.T[:, :, None])
        probability_gradient = jnp.einsum(
            "qhd,khd->hqk", lg, lv, preferred_element_type=jnp.float32
        )
        score_gradient = (probability * (probability_gradient - delta_rows.T[:, :, None])).astype(
            jnp.bfloat16
        )
        prob_b = probability.astype(jnp.bfloat16)
        query_grad = query_grad + spread_factor(
            softmax_scale
            * jnp.einsum("hqk,khd->qhd", score_gradient, lk, preferred_element_type=jnp.float32),
            dilation_rate,
            off,
        )
        grads_back.append((score_gradient, prob_b, lse_rows, delta_rows))
    dscore0, prob0, lse0, delta0 = grads_back[0]
    key_grad = softmax_scale * jnp.einsum(
        "hqk,qhd->khd", dscore0, query_full, preferred_element_type=jnp.float32
    )
    value_grad = jnp.einsum(
        "hqk,qhd->khd", prob0, gradient_full, preferred_element_type=jnp.float32
    )
    dscore1, prob1, lse1, delta1 = grads_back[1]
    mid_term = jnp.stack(
        [
            softmax_scale
            * jnp.einsum("hqk,qhd->khd", dscore1, middle_query, preferred_element_type=jnp.float32),
            jnp.einsum("hqk,qhd->khd", prob1, middle_gradient, preferred_element_type=jnp.float32),
        ],
        1,
    )
    middle_local_part = halved(
        mid_term,
        mid_bits,
        lambda piece, bit: partner(piece.astype(jnp.bfloat16), "ctx", bit).astype(piece.dtype),
        place_index,
    )
    dscore2, prob2, lse2, delta2 = grads_back[2]
    upper_local_part = lax.psum_scatter(
        jnp.stack(
            [
                softmax_scale
                * jnp.einsum(
                    "hqk,qhd->khd", dscore2, upper_query, preferred_element_type=jnp.float32
                ),
                jnp.einsum(
                    "hqk,qhd->khd", prob2, upper_gradient, preferred_element_type=jnp.float32
                ),
            ],
            1,
        ),
        "ctx",
        scatter_dimension=0,
        tiled=True,
    )
    key_grad = (
        key_grad
        + spread_factor(middle_local_part[:, 0], MIDDLE_DILATION, middle_offset)
        + spread_factor(upper_local_part[:, 0], UPPER_DILATION, upper_offset)
    )
    value_grad = (
        value_grad
        + spread_factor(middle_local_part[:, 1], MIDDLE_DILATION, middle_offset)
        + spread_factor(upper_local_part[:, 1], UPPER_DILATION, upper_offset)
    )
    flat = heads_dev * head_dim
    outputs = (
        attended.reshape(tok, flat),
        query_grad.astype(jnp.bfloat16).reshape(tok, flat),
        key_grad.astype(jnp.bfloat16).reshape(tok, flat),
        value_grad.astype(jnp.bfloat16).reshape(tok, flat),
    )
    attended_out, query_out, key_out, value_out = (
        lax.all_to_all(outputs[0], "head", split_axis=0, concat_axis=1, tiled=True),
        lax.all_to_all(outputs[1], "head", split_axis=0, concat_axis=1, tiled=True),
        lax.all_to_all(outputs[2], "head", split_axis=0, concat_axis=1, tiled=True),
        lax.all_to_all(outputs[3], "head", split_axis=0, concat_axis=1, tiled=True),
    )
    return (attended_out, query_out, key_out, value_out)


def solution(mesh):
    in_specs = (
        P(("ctx", "head"), None),
        P(("ctx", "head"), None),
        P(("ctx", "head"), None),
        P(("ctx", "head"), None),
        P(None, "head"),
    )
    out_specs = (
        P(("ctx", "head"), None),
        P(("ctx", "head"), None),
        P(("ctx", "head"), None),
        P(("ctx", "head"), None),
    )
    return jax.shard_map(local, mesh=mesh, in_specs=in_specs, out_specs=out_specs, check_vma=False)
```

profile of v0, /device:TPU:0, one launch (start us, length us, event | category | flops | bytes accessed | tf_op | source)
XLA Modules:
  0.0 312.5 jit_solution(9319243106495022859)
XLA Ops:
  9.5 4.2 %all-to-all-start.4 = ((bf16[128,4,1024]{2,0,1:T(8,128)(2,1)}), bf16[128,4,1024]{2,0,1:T(8,128)(2,1)S(1)}, u32[]{:S(2)}, u32[]{:S(2)}) async-start(bf16[128,4,1024]{2,0,1:T(8,128)(2,1)} %bitcast.258), calls=%async_computation.4 | async-start | bytes 2097152 | tf_op jit(solution)/shard_map/all_to_all | solution.py:76
  14.8 13.4 %all-to-all-done.4 = bf16[128,4,1024]{2,0,1:T(8,128)(2,1)S(1)} async-done(((bf16[128,4,1024]{2,0,1:T(8,128)(2,1)}), bf16[128,4,1024]{2,0,1:T(8,128)(2,1)S(1)}, u32[]{:S(2)}, u32[]{:S(2)}) %all-to-all-start.4) | async-done | bytes 1048608 | tf_op jit(solution)/shard_map/all_to_all | solution.py:76
  28.2 3.5 %all-to-all-start.1 = ((bf16[128,4,1024]{2,0,1:T(8,128)(2,1)}), bf16[128,4,1024]{2,0,1:T(8,128)(2,1)S(1)}, u32[]{:S(2)}, u32[]{:S(2)}) async-start(bf16[128,4,1024]{2,0,1:T(8,128)(2,1)} %bitcast.259), calls=%async_computation.1 | async-start | bytes 2097152 | tf_op jit(solution)/shard_map/all_to_all | solution.py:74
  32.8 13.4 %all-to-all-done.1 = bf16[128,4,1024]{2,0,1:T(8,128)(2,1)S(1)} async-done(((bf16[128,4,1024]{2,0,1:T(8,128)(2,1)}), bf16[128,4,1024]{2,0,1:T(8,128)(2,1)S(1)}, u32[]{:S(2)}, u32[]{:S(2)}) %all-to-all-start.1) | async-done | bytes 1048608 | tf_op jit(solution)/shard_map/all_to_all | solution.py:74
  46.2 3.5 %all-to-all-start.2 = ((bf16[128,4,1024]{2,0,1:T(8,128)(2,1)}), bf16[128,4,1024]{2,0,1:T(8,128)(2,1)S(1)}, u32[]{:S(2)}, u32[]{:S(2)}) async-start(bf16[128,4,1024]{2,0,1:T(8,128)(2,1)} %bitcast.291), calls=%async_computation.2 | async-start | bytes 2097152 | tf_op jit(solution)/shard_map/all_to_all | solution.py:75
  52.0 12.1 %all-to-all-done.2 = bf16[128,4,1024]{2,0,1:T(8,128)(2,1)S(1)} async-done(((bf16[128,4,1024]{2,0,1:T(8,128)(2,1)}), bf16[128,4,1024]{2,0,1:T(8,128)(2,1)S(1)}, u32[]{:S(2)}, u32[]{:S(2)}) %all-to-all-start.2) | async-done | bytes 1048608 | tf_op jit(solution)/shard_map/all_to_all | solution.py:75
  64.1 4.2 %all-to-all-start = ((bf16[128,4,1024]{2,0,1:T(8,128)(2,1)}), bf16[128,4,1024]{2,0,1:T(8,128)(2,1)}, u32[]{:S(2)}, u32[]{:S(2)}) async-start(bf16[128,4,1024]{2,0,1:T(8,128)(2,1)} %bitcast.289), calls=%async_computation | async-start | bytes 2097152 | tf_op jit(solution)/shard_map/all_to_all | solution.py:73
  74.0 8.9 %all-to-all-done = bf16[128,4,1024]{2,0,1:T(8,128)(2,1)} async-done(((bf16[128,4,1024]{2,0,1:T(8,128)(2,1)}), bf16[128,4,1024]{2,0,1:T(8,128)(2,1)}, u32[]{:S(2)}, u32[]{:S(2)}) %all-to-all-start) | async-done | bytes 1048608 | tf_op jit(solution)/shard_map/all_to_all | solution.py:73
  86.0 27.9 %all_gather.3 = bf16[2,64,8,128]{3,1,2,0:T(8,128)(2,1)S(1)} all-gather(bf16[2,8,8,128]{3,1,2,0:T(8,128)(2,1)S(1)} %pad_maximum_fusion.3), channel_id=1, replica_groups=mesh['ctx'=8,'head'=4] {'ctx'}, dimensions={1}, use_global_device_ids=true | all-gather | bytes 294912 | tf_op jit(solution)/shard_map/all_gather | solution.py:109
  117.5 4.5 %multiply_reduce_fusion = (f32[8,512]{1,0:T(8,128)S(1)}, f32[8,512,512]{1,2,0:T(8,128)}) fusion(bf16[512,8,128]{2,1,0:T(8,128)(2,1)S(1)} %bitcast.270, bf16[512,8,128]{2,1,0:T(8,128)(2,1)S(1)} %bitcast.266), kind=kOutput, calls=%fused_computation.6 | convolution fusion | flops 541061120 | bytes 10502144 | tf_op jit(solution)/shard_map/qhd,khd->hqk/dot_general | solution.py:130
  133.1 4.8 %fusion = f32[8,512]{1,0:T(8,128)S(1)} fusion(f32[8,512,512]{1,2,0:T(8,128)} %get-tuple-element.39, f32[8,512]{1,0:T(8,128)S(1)} %bitcast.300), kind=kLoop, calls=%fused_computation.3 | loop fusion | flops 6287360 | bytes 8421376 | tf_op jit(solution)/shard_map/reduce_sum | solution.py:143
  145.9 3.0 copy.212
  148.9 8.6 %multiply_reduce_fusion.1 = (f32[512,8]{0,1:T(8,128)}, bf16[512,8,128]{0,2,1:T(8,128)(2,1)}) fusion(bf16[512,8,128]{0,2,1:T(8,128)(2,1)S(1)} %copy-done.3, f32[512,8]{0,1:T(8,128)} %get-tuple-element.31, f32[512,8,128]{0,2,1:T(8,128)} %copy.216, pred[512,8]{0,1:T(8,128)(4,1)} %broadcast_in_dim.279, f32[512,8,128]{0,2,1:T(8,128)} %copy.212, ...), kind=kOutput, calls=%fused_computation.26 | convolution fusion | flops 548401152 | bytes 15785984 | tf_op jit(solution)/shard_map/hqk,khd->qhd/dot_general | solution.py:144
  177.1 4.2 %all-to-all-start.3 = ((bf16[4,128,1024]{1,2,0:T(8,128)(2,1)}), bf16[4,128,1024]{1,2,0:T(8,128)(2,1)}, u32[]{:S(2)}, u32[]{:S(2)}) async-start(bf16[4,128,1024]{1,2,0:T(8,128)(2,1)} %copy.217), calls=%async_computation.3 | async-start | bytes 2097152 | tf_op jit(solution)/shard_map/all_to_all | solution.py:233
  195.0 5.2 %multiply_convert_fusion = bf16[8,512,512]{1,2,0:T(8,128)(2,1)S(1)} fusion(f32[8,512,512]{1,2,0:T(8,128)} %get-tuple-element.39, f32[8,512]{1,0:T(8,128)S(1)} %bitcast.298, f32[8,512]{1,0:T(8,128)S(1)} %bitcast.296, bf16[512,8,128]{0,2,1:T(8,128)(2,1)S(1)} %copy-done.3, bf16[512,8,128]{0,2,1:T(8,128)(2,1)} %copy.264), kind=kOutput, calls=%fused_computation | convolution fusion | flops 547356672 | bytes 14712832 | tf_op jit(solution)/shard_map/qhd,khd->hqk/dot_general | solution.py:161
  216.7 4.3 %all-to-all-start.5 = ((bf16[4,128,1024]{1,2,0:T(8,128)(2,1)}), bf16[4,128,1024]{1,2,0:T(8,128)(2,1)}, u32[]{:S(2)}, u32[]{:S(2)}) async-start(bf16[4,128,1024]{1,2,0:T(8,128)(2,1)} %copy.232), calls=%async_computation.5 | async-start | bytes 2097152 | tf_op jit(solution)/shard_map/all_to_all | solution.py:234
  221.0 32.8 %reduce-scatter.2.cloned.1.call-done = f32[8,2,8,128]{3,0,2,1:T(8,128)} async-done(((f32[64,2,8,128]{3,0,2,1:T(8,128)}), f32[8,2,8,128]{3,0,2,1:T(8,128)}) %reduce-scatter.2.cloned.1.call-update) | async-done | bytes 65552 | tf_op jit(solution)/shard_map/reduce_scatter | solution.py:198
  256.0 3.0 copy.242
  259.0 5.1 %fusion.14 = bf16[512,8,128]{0,2,1:T(8,128)(2,1)S(1)} fusion(f32[512,8,128]{0,2,1:T(8,128)} %copy.242, f32[512,8,128]{0,2,1:T(8,128)} %copy.238, bf16[8,512,512]{1,2,0:T(8,128)(2,1)} %copy-done, pred[512,8]{0,1:T(8,128)(4,1)S(1)} %copy-done.19, pred[512,8]{0,1:T(8,128)(4,1)S(1)} %copy-done.21, bf16[512,8,128]{2,1,0:T(8,128)(2,1)S(1)} %bitcast.267), kind=kOutput, calls=%fused_computation.18 | convolution fusion | flops 540016640 | bytes 10493952 | tf_op jit(solution)/shard_map/hqk,qhd->khd/dot_general | solution.py:176
  267.5 4.4 %all-to-all-start.6 = ((bf16[4,128,1024]{1,2,0:T(8,128)(2,1)}), bf16[4,128,1024]{1,2,0:T(8,128)(2,1)}, u32[]{:S(2)}, u32[]{:S(2)}) async-start(bf16[4,128,1024]{1,2,0:T(8,128)(2,1)} %copy.243), calls=%async_computation.7 | async-start | bytes 2097152 | tf_op jit(solution)/shard_map/all_to_all | solution.py:235
  271.9 6.9 %fusion.12 = bf16[512,8,128]{0,2,1:T(8,128)(2,1)} fusion(f32[512,8,128]{0,2,1:T(8,128)} %copy.249, f32[512,8,128]{0,2,1:T(8,128)S(1)} %copy-done.4, bf16[512,8,128]{0,2,1:T(8,128)(2,1)S(1)} %copy-done.3, f32[8,512,512]{1,2,0:T(8,128)} %get-tuple-element.39, f32[8,512]{1,0:T(8,128)S(1)} %bitcast.297, pred[512,8]{0,1:T(8,128)(4,1)S(1)} %copy-done.19, ...), kind=kOutput, calls=%fused_computation.15 | convolution fusion | flops 545783808 | bytes 14704640 | tf_op jit(solution)/shard_map/hqk,qhd->khd/dot_general | solution.py:179
  281.3 5.1 %all-to-all-done.6 = bf16[4,128,1024]{1,2,0:T(8,128)(2,1)} async-done(((bf16[4,128,1024]{1,2,0:T(8,128)(2,1)}), bf16[4,128,1024]{1,2,0:T(8,128)(2,1)}, u32[]{:S(2)}, u32[]{:S(2)}) %all-to-all-start.6) | async-done | bytes 1048608 | tf_op jit(solution)/shard_map/all_to_all | solution.py:235
  286.4 3.5 %all-to-all-start.7 = ((bf16[4,128,1024]{1,2,0:T(8,128)(2,1)}), bf16[4,128,1024]{1,2,0:T(8,128)(2,1)S(1)}, u32[]{:S(2)}, u32[]{:S(2)}) async-start(bf16[4,128,1024]{1,2,0:T(8,128)(2,1)} %copy.250), calls=%async_computation.8 | async-start | bytes 2097152 | tf_op jit(solution)/shard_map/all_to_all | solution.py:236
  296.7 7.6 %all-to-all-done.7 = bf16[4,128,1024]{1,2,0:T(8,128)(2,1)S(1)} async-done(((bf16[4,128,1024]{1,2,0:T(8,128)(2,1)}), bf16[4,128,1024]{1,2,0:T(8,128)(2,1)S(1)}, u32[]{:S(2)}, u32[]{:S(2)}) %all-to-all-start.7) | async-done | bytes 1048608 | tf_op jit(solution)/shard_map/all_to_all | solution.py:236
  (167 shorter events, 103.7 us)
Async XLA Ops:
  7.2 6.6 %copy-start.11 = (bf16[128,4096]{1,0:T(8,128)(2,1)S(1)}, bf16[128,4096]{1,0:T(8,128)(2,1)}, u32[]{:S(2)}) copy-start(bf16[128,4096]{1,0:T(8,128)(2,1)} %param.6) | copy-start | bytes 3145732
  9.5 18.7 %all-to-all-start.4 = ((bf16[128,4,1024]{2,0,1:T(8,128)(2,1)}), bf16[128,4,1024]{2,0,1:T(8,128)(2,1)S(1)}, u32[]{:S(2)}, u32[]{:S(2)}) async-start(bf16[128,4,1024]{2,0,1:T(8,128)(2,1)} %bitcast.258), calls=%async_computation.4 | async-start | bytes 2097152 | tf_op jit(solution)/shard_map/all_to_all | solution.py:76
  14.8 16.9 %copy-start.12 = (bf16[128,4096]{1,0:T(8,128)(2,1)S(1)}, bf16[128,4096]{1,0:T(8,128)(2,1)}, u32[]{:S(2)}) copy-start(bf16[128,4096]{1,0:T(8,128)(2,1)} %param.7) | copy-start | bytes 3145732
  28.2 18.0 %all-to-all-start.1 = ((bf16[128,4,1024]{2,0,1:T(8,128)(2,1)}), bf16[128,4,1024]{2,0,1:T(8,128)(2,1)S(1)}, u32[]{:S(2)}, u32[]{:S(2)}) async-start(bf16[128,4,1024]{2,0,1:T(8,128)(2,1)} %bitcast.259), calls=%async_computation.1 | async-start | bytes 2097152 | tf_op jit(solution)/shard_map/all_to_all | solution.py:74
  46.2 18.0 %all-to-all-start.2 = ((bf16[128,4,1024]{2,0,1:T(8,128)(2,1)}), bf16[128,4,1024]{2,0,1:T(8,128)(2,1)S(1)}, u32[]{:S(2)}, u32[]{:S(2)}) async-start(bf16[128,4,1024]{2,0,1:T(8,128)(2,1)} %bitcast.291), calls=%async_computation.2 | async-start | bytes 2097152 | tf_op jit(solution)/shard_map/all_to_all | solution.py:75
  49.7 18.7 %copy-start.26 = (s32[2,8]{1,0:T(2,128)S(1)}, s32[2,8]{1,0:T(2,128)}, u32[]{:S(2)}) copy-start(s32[2,8]{1,0:T(2,128)} %param.9) | copy-start | bytes 196
  64.1 6.6 %copy-start.7 = (bf16[128,4,1024]{2,0,1:T(8,128)(2,1)}, bf16[128,4,1024]{2,0,1:T(8,128)(2,1)S(1)}, u32[]{:S(2)}) copy-start(bf16[128,4,1024]{2,0,1:T(8,128)(2,1)S(1)} %all-to-all-done.2) | copy-start | bytes 3145732
  64.1 18.8 %all-to-all-start = ((bf16[128,4,1024]{2,0,1:T(8,128)(2,1)}), bf16[128,4,1024]{2,0,1:T(8,128)(2,1)}, u32[]{:S(2)}, u32[]{:S(2)}) async-start(bf16[128,4,1024]{2,0,1:T(8,128)(2,1)} %bitcast.289), calls=%async_computation | async-start | bytes 2097152 | tf_op jit(solution)/shard_map/all_to_all | solution.py:73
  86.0 36.0 %copy-start.15 = (bf16[8,8,128]{2,1,0:T(8,128)(2,1)}, bf16[8,8,128]{2,1,0:T(8,128)(2,1)S(1)}, u32[]{:S(2)}) copy-start(bf16[8,8,128]{2,1,0:T(8,128)(2,1)S(1)} %get-tuple-element.21) | copy-start | bytes 49156
  114.0 8.0 %copy-start.14 = (bf16[2,64,8,128]{3,1,2,0:T(8,128)(2,1)}, bf16[2,64,8,128]{3,1,2,0:T(8,128)(2,1)S(1)}, u32[]{:S(2)}) copy-start(bf16[2,64,8,128]{3,1,2,0:T(8,128)(2,1)S(1)} %all_gather.3) | copy-start | bytes 786436
  116.2 10.3 %collective-permute-start = (bf16[2,32,8,128]{3,1,2,0:T(8,128)(2,1)S(1)}, bf16[2,32,8,128]{3,1,2,0:T(8,128)(2,1)}, u32[]{:S(2)}, u32[]{:S(2)}) collective-permute-start(bf16[2,32,8,128]{3,1,2,0:T(8,128)(2,1)S(1)} %pad_maximum_fusion.2), channel_id=1, source_target_pairs={{0,4},{4,0},{8,12},{12,8},{16,20},{20,16},{24,28},{28,24},{1,5},{5... | collective-permute-start | bytes 393224 | tf_op jit(solution)/shard_map/ppermute | solution.py:17
  126.5 6.6 %copy-start.22 = (f32[512,8]{0,1:T(8,128)S(1)}, f32[512,8]{0,1:T(8,128)}, u32[]{:S(2)}) copy-start(f32[512,8]{0,1:T(8,128)} %max.41) | copy-start | bytes 49156
  160.4 11.3 %copy-start.13 = (bf16[32,8,128]{2,1,0:T(8,128)(2,1)S(1)}, bf16[32,8,128]{2,1,0:T(8,128)(2,1)}, u32[]{:S(2)}) copy-start(bf16[32,8,128]{2,1,0:T(8,128)(2,1)} %get-tuple-element.25) | copy-start | bytes 196612
  174.7 6.9 %copy-start.23 = (f32[8,8,128]{2,0,1:T(8,128)S(1)}, f32[8,8,128]{2,0,1:T(8,128)}, u32[]{:S(2)}) copy-start(f32[8,8,128]{2,0,1:T(8,128)} %fusion.29) | copy-start | bytes 98308
  177.1 39.6 %all-to-all-start.3 = ((bf16[4,128,1024]{1,2,0:T(8,128)(2,1)}), bf16[4,128,1024]{1,2,0:T(8,128)(2,1)}, u32[]{:S(2)}, u32[]{:S(2)}) async-start(bf16[4,128,1024]{1,2,0:T(8,128)(2,1)} %copy.217), calls=%async_computation.3 | async-start | bytes 2097152 | tf_op jit(solution)/shard_map/all_to_all | solution.py:233
  181.3 72.4 %reduce-scatter.2.cloned.1.call-start = ((), (), s32[]{:S(2)}) async-start(), calls=%async_computation.9 | async-start | bytes 589824 | tf_op jit(solution)/shard_map/reduce_scatter | solution.py:198
  194.2 12.5 %collective-permute-start.1 = (bf16[32,2,8,128]{3,0,2,1:T(8,128)(2,1)}, bf16[32,2,8,128]{3,0,2,1:T(8,128)(2,1)}, u32[]{:S(2)}, u32[]{:S(2)}) collective-permute-start(bf16[32,2,8,128]{3,0,2,1:T(8,128)(2,1)} %select_convert_fusion), channel_id=1, source_target_pairs={{0,4},{4,0},{8,12},{12,8},{16,20},{20,16},{24,28},{28,24},{1,5},{5... | collective-permute-start | bytes 393224 | tf_op jit(solution)/shard_map/ppermute | solution.py:17
  195.0 7.2 %copy-start.5 = (f32[512,8,128]{0,2,1:T(8,128)S(1)}, f32[512,8,128]{0,2,1:T(8,128)}, u32[]{:S(2)}) copy-start(f32[512,8,128]{0,2,1:T(8,128)} %copy.231) | copy-start | bytes 6291460
  195.0 7.2 %copy-start.6 = (f32[512,8,128]{0,2,1:T(8,128)S(1)}, f32[512,8,128]{0,2,1:T(8,128)}, u32[]{:S(2)}) copy-start(f32[512,8,128]{0,2,1:T(8,128)} %copy.228) | copy-start | bytes 6291460
  195.0 7.2 %copy-start.19 = (pred[512,8]{0,1:T(8,128)(4,1)S(1)}, pred[512,8]{0,1:T(8,128)(4,1)}, u32[]{:S(2)}) copy-start(pred[512,8]{0,1:T(8,128)(4,1)} %broadcast_in_dim.279) | copy-start | bytes 12292
  195.0 7.2 %copy-start.21 = (pred[512,8]{0,1:T(8,128)(4,1)S(1)}, pred[512,8]{0,1:T(8,128)(4,1)}, u32[]{:S(2)}) copy-start(pred[512,8]{0,1:T(8,128)(4,1)} %broadcast_in_dim.281) | copy-start | bytes 12292
  216.7 50.8 %all-to-all-start.5 = ((bf16[4,128,1024]{1,2,0:T(8,128)(2,1)}), bf16[4,128,1024]{1,2,0:T(8,128)(2,1)}, u32[]{:S(2)}, u32[]{:S(2)}) async-start(bf16[4,128,1024]{1,2,0:T(8,128)(2,1)} %copy.232), calls=%async_computation.5 | async-start | bytes 2097152 | tf_op jit(solution)/shard_map/all_to_all | solution.py:234
  267.5 18.9 %all-to-all-start.6 = ((bf16[4,128,1024]{1,2,0:T(8,128)(2,1)}), bf16[4,128,1024]{1,2,0:T(8,128)(2,1)}, u32[]{:S(2)}, u32[]{:S(2)}) async-start(bf16[4,128,1024]{1,2,0:T(8,128)(2,1)} %copy.243), calls=%async_computation.7 | async-start | bytes 2097152 | tf_op jit(solution)/shard_map/all_to_all | solution.py:235
  286.4 18.0 %all-to-all-start.7 = ((bf16[4,128,1024]{1,2,0:T(8,128)(2,1)}), bf16[4,128,1024]{1,2,0:T(8,128)(2,1)S(1)}, u32[]{:S(2)}, u32[]{:S(2)}) async-start(bf16[4,128,1024]{1,2,0:T(8,128)(2,1)} %copy.250), calls=%async_computation.8 | async-start | bytes 2097152 | tf_op jit(solution)/shard_map/all_to_all | solution.py:236
  (14 other events, 46.1 us)
Sparse Core Ops, SparseCore 0:
  192.7 61.0 reduce-scatter.1
where the time goes:
time: 314 us; the launch traced here: 313 us
  waiting for transfers between devices  93.3 us (30%)
  local copies, waits for them, and re-layouts  77.8 us (25%)
  matrix products  45.7 us (15%)
  starting transfers between devices  34.2 us (11%)
  blocking collectives  27.9 us (9%)
  other arithmetic  19 us (6%)
  between operations  14.6 us (5%)
    broadcast_in_dim x26, local copies, waits for them, and re-layouts, spread_factor(): full = jnp.where(mask, rows[:, None], jnp.zeros((), rows.dtype))  34.5 us
    reduce_scatter x1, waiting for transfers between devices, local(): lax.psum_scatter(jnp.stack([softmax_scale * jnp.einsum('hqk,qhd->khd', ds...  32.8 us
    all_gather x1, blocking collectives, local(): upper_key_rows = lax.all_gather(upper_owned_rows, 'ctx', axis=1, tiled=True)  27.9 us
    unnamed x62, local copies, waits for them, and re-layouts  13.5 us
    all_to_all x1, waiting for transfers between devices, local(): lax.all_to_all(out_grad, 'head', split_axis=1, concat_axis=0, tiled=True)  13.4 us
    all_to_all x1, waiting for transfers between devices, local(): lax.all_to_all(key, 'head', split_axis=1, concat_axis=0, tiled=True)  13.4 us
    all_to_all x1, waiting for transfers between devices, local(): lax.all_to_all(value, 'head', split_axis=1, concat_axis=0, tiled=True)  12.1 us
    dot_general x3, matrix products, local(): jnp.einsum('hqk,khd->qhd', level_weight.astype(jnp.bfloat16), lv, preferr...  9.99 us
  transfers between devices with their start and end apart: 11, of which 7 were waited for; matrix products, arithmetic and copies ran while one was open for 25% of the time, Pallas kernels for 0%

commit v1 on v0

v1 whole, which is shorter than its diff:
```python
import functools
import math

import jax
import jax.numpy as jnp
from jax import lax
from jax.experimental import pallas as pl
from jax.experimental.pallas import tpu as pltpu
from jax.sharding import PartitionSpec as P

MIDDLE_DILATION = 16
UPPER_DILATION = 64
MIDDLE_SEGMENTS = 4
LOWEST = -1e30
MESH = pl.DeviceIdType.MESH
F32 = jnp.float32
BF16 = jnp.bfloat16


def contract(a, b, dim_a, dim_b):
    return lax.dot_general(a, b, (((dim_a,), (dim_b,)), ((), ())), preferred_element_type=F32)


def one_hot(shape, row_dim, tok, middle_offset, upper_offset, copies):
    mid_rows, top_rows = tok // MIDDLE_DILATION, tok // UPPER_DILATION
    rows = lax.broadcasted_iota(jnp.int32, shape, row_dim)
    token = lax.broadcasted_iota(jnp.int32, shape, 1 - row_dim)
    if copies > 1:
        rows = jnp.where(rows >= mid_rows + top_rows, rows - (mid_rows + top_rows), rows)
    owner = jnp.where(
        rows < mid_rows,
        rows * MIDDLE_DILATION + middle_offset,
        (rows - mid_rows) * UPPER_DILATION + upper_offset,
    )
    return jnp.where(token == owner, 1.0, 0.0).astype(BF16)


def kernel(
    dims,
    offsets, query, key, value, out_grad,
    attended_out, query_out, key_out, value_out,
    arrived, staged, partial,
    mid_own, mid_rows_in, top_own, top_rows_in,
    mid_back, mid_back_in, top_back, top_back_in,
    in_recv, mid_recv, top_recv, mid_back_recv, top_back_recv, out_recv,
    in_send, mid_send, top_send, mid_back_send, top_back_send, out_send,
):
    ctx_count, mid_count, group, heads, own_rows, width = dims
    tok = own_rows * group
    mid_n, top_n = tok // MIDDLE_DILATION, tok // UPPER_DILATION
    ctx, me = lax.axis_index("ctx"), lax.axis_index("head")
    mid_base = ctx // mid_count * mid_count
    mid_me = ctx % mid_count
    sources = (query, key, value, out_grad)
    results = (attended_out, query_out, key_out, value_out)
    scale = width ** -0.5

    barrier = pltpu.get_barrier_semaphore()
    for step in range(1, group):
        pl.semaphore_signal(barrier, inc=1, device_id={"head": (me + step) % group}, device_id_type=MESH)

    def greet(step, carry):
        pl.semaphore_signal(barrier, inc=1, device_id={"ctx": (ctx + step) % ctx_count}, device_id_type=MESH)
        return carry

    lax.fori_loop(1, ctx_count, greet, 0)
    pl.semaphore_wait(barrier, group - 1 + ctx_count - 1)

    def columns(device, head):
        return pl.ds(pl.multiple_of((device * heads + head) * width, width), width)

    def rows_of(device):
        return pl.ds(pl.multiple_of(device * own_rows, own_rows), own_rows)

    def send_in(head, carry):
        for step in range(group):
            device = (me + step) % group
            for a in (1, 2, 0, 3):
                src = sources[a].at[:, columns(device, head)]
                dst = arrived.at[head, a, rows_of(me)]
                if step == 0:
                    pltpu.make_async_copy(src, dst, in_recv.at[head]).start()
                else:
                    pltpu.make_async_remote_copy(
                        src, dst, in_send.at[a], in_recv.at[head],
                        device_id={"head": device}, device_id_type=MESH,
                    ).start()
        return carry

    lax.fori_loop(0, heads, send_in, 0)

    def ring(count, place, base, src_of, dst, send_sem, recv_sem):
        def body(step, carry):
            other = (place + step) % count
            pltpu.make_async_remote_copy(
                src_of(other), dst, send_sem, recv_sem,
                device_id={"ctx": base + other}, device_id_type=MESH,
            ).start()
            return carry

        lax.fori_loop(1, count, body, 0)

    def wait_for(ref, sem):
        pltpu.make_async_copy(ref, ref, sem).wait()

    def gather_rows(head):
        wait_for(arrived.at[head], in_recv.at[head])
        pick = one_hot((mid_n + top_n, tok), 0, tok, offsets[0, head], offsets[1, head], 1)
        key_rows = contract(pick, arrived[head, 1], 1, 0)
        value_rows = contract(pick, arrived[head, 2], 1, 0)
        mid = jnp.concatenate([key_rows[:mid_n], value_rows[:mid_n]], 0).astype(BF16)
        top = jnp.concatenate([key_rows[mid_n:], value_rows[mid_n:]], 0).astype(BF16)
        mid_own[head] = mid
        top_own[head] = top
        mid_rows_in[head, mid_me] = mid
        top_rows_in[head, ctx] = top
        ring(ctx_count, ctx, 0, lambda other: top_own.at[head], top_rows_in.at[head, ctx],
             top_send, top_recv.at[head])
        ring(mid_count, mid_me, mid_base, lambda other: mid_own.at[head], mid_rows_in.at[head, mid_me],
             mid_send, mid_recv.at[head])

    def send_out(head, a):
        for step in range(group):
            device = (me + step) % group
            src = staged.at[head, a, rows_of(device)]
            dst = results[a].at[:, columns(me, head)]
            if step == 0:
                pltpu.make_async_copy(src, dst, out_recv.at[a]).start()
            else:
                pltpu.make_async_remote_copy(
                    src, dst, out_send.at[a], out_recv.at[a],
                    device_id={"head": device}, device_id_type=MESH,
                ).start()

    def attend(head):
        wait_for(mid_rows_in.at[head, pl.ds(0, mid_count - 1)], mid_recv.at[head])
        wait_for(top_rows_in.at[head, pl.ds(0, ctx_count - 1)], top_recv.at[head])
        mid_in = mid_rows_in[head].astype(F32)
        top_in = top_rows_in[head].astype(F32)
        mid_all, top_all = mid_count * mid_n, ctx_count * top_n
        q, do = arrived[head, 0], arrived[head, 3]
        k = jnp.concatenate([
            arrived[head, 1],
            mid_in[:, :mid_n].reshape(mid_all, width).astype(BF16),
            top_in[:, :top_n].reshape(top_all, width).astype(BF16),
        ], 0)
        v = jnp.concatenate([
            arrived[head, 2],
            mid_in[:, mid_n:].reshape(mid_all, width).astype(BF16),
            top_in[:, top_n:].reshape(top_all, width).astype(BF16),
        ], 0)
        position = lax.broadcasted_iota(jnp.int32, (1, tok), 1)
        in_mid = position % MIDDLE_DILATION == offsets[0, head]
        in_top = position % UPPER_DILATION == offsets[1, head]
        score = contract(k, q, 1, 1) * (scale * math.log2(math.e))
        score = jnp.concatenate([
            score[:tok],
            jnp.where(in_mid, score[tok:tok + mid_all], LOWEST),
            jnp.where(in_top, score[tok + mid_all:], LOWEST),
        ], 0)
        top = jnp.max(score, 0, keepdims=True)
        weight = jnp.exp2(score - top)
        inverse = 1.0 / jnp.sum(weight, 0, keepdims=True)
        attended = (contract(v, weight.astype(BF16), 0, 0) * inverse).astype(BF16).astype(F32)
        delta = jnp.sum(do.astype(F32).T * attended, 0, keepdims=True)
        prob = weight * inverse
        dscore = (prob * (contract(v, do, 1, 1) - delta)).astype(BF16)
        staged[head, 0] = attended.T.astype(BF16)
        send_out(head, 0)
        staged[head, 1] = (contract(k, dscore, 0, 0) * scale).T.astype(BF16)
        send_out(head, 1)
        dk = contract(dscore, q, 1, 0) * scale
        dv = contract(prob.astype(BF16), do, 1, 0)
        partial[head % 2, 0] = dk[:tok]
        partial[head % 2, 1] = dv[:tok]

        def both(low, count, n):
            return jnp.concatenate([
                dk[low:low + count * n].reshape(count, n, width),
                dv[low:low + count * n].reshape(count, n, width),
            ], 1).astype(BF16)

        mid_back[head] = both(tok, mid_count, mid_n)
        top_back[head] = both(tok + mid_all, ctx_count, top_n)
        ring(ctx_count, ctx, 0, lambda other: top_back.at[head, other], top_back_in.at[head, ctx],
             top_back_send, top_back_recv.at[head])
        ring(mid_count, mid_me, mid_base, lambda other: mid_back.at[head, other], mid_back_in.at[head, mid_me],
             mid_back_send, mid_back_recv.at[head])
        top_back_in[head, ctx] = top_back[head, ctx]
        mid_back_in[head, mid_me] = mid_back[head, mid_me]

    def finish(head):
        wait_for(mid_back_in.at[head, pl.ds(0, mid_count - 1)], mid_back_recv.at[head])
        wait_for(top_back_in.at[head, pl.ds(0, ctx_count - 1)], top_back_recv.at[head])
        mid = jnp.sum(mid_back_in[head].astype(F32), 0)
        top = jnp.sum(top_back_in[head].astype(F32), 0)
        rows = jnp.concatenate([
            jnp.concatenate([mid[:mid_n], top[:top_n]], 0),
            jnp.concatenate([mid[mid_n:], top[top_n:]], 0),
        ], 1)
        high = rows.astype(BF16).astype(F32)
        both = jnp.concatenate([high, rows - high], 0).astype(BF16)
        place = one_hot((tok, 2 * (mid_n + top_n)), 1, tok, offsets[0, head], offsets[1, head], 2)
        added = contract(place, both, 1, 0)
        staged[head, 2] = (partial[head % 2, 0] + added[:, :width]).astype(BF16)
        send_out(head, 2)
        staged[head, 3] = (partial[head % 2, 1] + added[:, width:]).astype(BF16)
        send_out(head, 3)

    gather_rows(0)

    def turn(head, carry):
        @pl.when(head < heads - 1)
        def _():
            gather_rows(head + 1)

        attend(head)

        @pl.when(head > 0)
        def _():
            finish(head - 1)

        return carry

    lax.fori_loop(0, heads, turn, 0)
    finish(heads - 1)

    others = pl.ds(0, own_rows * (group - 1))
    for a in range(4):
        wait_for(results[a], out_recv.at[a])
        wait_for(staged.at[:, a, others], out_send.at[a])
        wait_for(arrived.at[:, a, others], in_send.at[a])
    wait_for(mid_rows_in.at[:, pl.ds(0, mid_count - 1)], mid_send)
    wait_for(top_rows_in.at[:, pl.ds(0, ctx_count - 1)], top_send)
    wait_for(mid_back_in.at[:, pl.ds(0, mid_count - 1)], mid_back_send)
    wait_for(top_back_in.at[:, pl.ds(0, ctx_count - 1)], top_back_send)


def local(query, key, value, out_grad, offsets):
    ctx_count, group = lax.axis_size("ctx"), lax.axis_size("head")
    heads = offsets.shape[1]
    own_rows = query.shape[0]
    width = query.shape[1] // (group * heads)
    tok = own_rows * group
    mid_count = ctx_count // MIDDLE_SEGMENTS
    mid_n, top_n = tok // MIDDLE_DILATION, tok // UPPER_DILATION
    dims = (ctx_count, mid_count, group, heads, own_rows, width)
    anywhere = pl.BlockSpec(memory_space=pl.ANY)
    dma = pltpu.SemaphoreType.DMA
    return pl.pallas_call(
        functools.partial(kernel, dims),
        out_shape=tuple(jax.ShapeDtypeStruct(query.shape, BF16) for _ in range(4)),
        in_specs=[pl.BlockSpec(memory_space=pltpu.SMEM)] + [anywhere] * 4,
        out_specs=(anywhere,) * 4,
        scratch_shapes=[
            pltpu.VMEM((heads, 4, tok, width), BF16),
            pltpu.VMEM((heads, 4, tok, width), BF16),
            pltpu.VMEM((2, 2, tok, width), F32),
            pltpu.VMEM((heads, 2 * mid_n, width), BF16),
            pltpu.VMEM((heads, mid_count, 2 * mid_n, width), BF16),
            pltpu.VMEM((heads, 2 * top_n, width), BF16),
            pltpu.VMEM((heads, ctx_count, 2 * top_n, width), BF16),
            pltpu.VMEM((heads, mid_count, 2 * mid_n, width), BF16),
            pltpu.VMEM((heads, mid_count, 2 * mid_n, width), BF16),
            pltpu.VMEM((heads, ctx_count, 2 * top_n, width), BF16),
            pltpu.VMEM((heads, ctx_count, 2 * top_n, width), BF16),
            dma((heads,)), dma((heads,)), dma((heads,)), dma((heads,)), dma((heads,)), dma((4,)),
            dma((4,)), dma, dma, dma, dma, dma((4,)),
        ],
        compiler_params=pltpu.CompilerParams(
            collective_id=0, has_side_effects=True, vmem_limit_bytes=56 * 1024 * 1024
        ),
        cost_estimate=pl.CostEstimate(
            flops=12 * heads * tok * (tok + 128) * width,
            bytes_accessed=16 * query.size,
            transcendentals=heads * tok * (tok + 128),
        ),
        name="dilated_attention",
    )(offsets, query, key, value, out_grad)


def solution(mesh):
    rows = P(("ctx", "head"), None)
    return jax.shard_map(
        local, mesh=mesh, in_specs=(rows,) * 4 + (P(None, "head"),), out_specs=(rows,) * 4, check_vma=False
    )
```

time: 314 us -> 106 us (0.34)
  Pallas kernels: 0 us -> 99 us
  waiting for transfers between devices: 93.3 us -> 0 us
  local copies, waits for them, and re-layouts: 77.8 us -> 6.55 us
  matrix products: 45.7 us -> 0 us
  starting transfers between devices: 34.2 us -> 0 us
  blocking collectives: 27.9 us -> 0 us
  other arithmetic: 19 us -> 0 us
  between operations: 14.6 us -> 0.65 us
    pallas_call x0 -> x1, Pallas kernels: none -> 99 us  [local(): pl.pallas_call(functools.partial(kernel, dims), out_shape=tuple((jax.Shap...]
    all_to_all x8 -> x0, waiting for transfers between devices: 60.6 us -> none  [the longest x1 13.4 us: local(): lax.all_to_all(out_grad, 'head', split_axis=1, concat_axis=0, tiled=True)]
    dot_general x18 -> x0, matrix products: 45.7 us -> none  [the longest x3 9.99 us: local(): jnp.einsum('hqk,khd->qhd', level_weight.astype(jnp.bfloat16), lv, preferr...]
    broadcast_in_dim x31 -> x0, local copies, waits for them, and re-layouts: 36.6 us -> none  [the longest x26 34.5 us: spread_factor(): full = jnp.where(mask, rows[:, None], jnp.zeros((), rows.dtype))]
    reduce_scatter x1 -> x0, waiting for transfers between devices: 32.8 us -> none  [local(): lax.psum_scatter(jnp.stack([softmax_scale * jnp.einsum('hqk,qhd->khd', ds...]
    all_to_all x8 -> x0, starting transfers between devices: 31.9 us -> none  [the longest x1 4.4 us: local(): lax.all_to_all(outputs[2], 'head', split_axis=0, concat_axis=1, tiled=True)]
    all_gather x1 -> x0, blocking collectives: 27.9 us -> none  [local(): upper_key_rows = lax.all_gather(upper_owned_rows, 'ctx', axis=1, tiled=True)]
    all_to_all x12 -> x0, local copies, waits for them, and re-layouts: 17.5 us -> none  [the longest x2 4.47 us: local(): lax.all_to_all(outputs[0], 'head', split_axis=0, concat_axis=1, tiled=True)]
  transfers between devices with their start and end apart: 11 -> 0, of which waited for: 7 -> 0; matrix products, arithmetic and copies ran while one was open for 25% -> 0% of each run, Pallas kernels for 0% -> 0%
where the time goes in v1:
time: 106 us
  Pallas kernels  99 us (93%)
  local copies, waits for them, and re-layouts  6.55 us (6%)
    pallas_call x1, Pallas kernels, local(): pl.pallas_call(functools.partial(kernel, dims), out_shape=tuple((jax.Shap...  99 us
    unnamed x10, local copies, waits for them, and re-layouts  6.55 us

profile of v1, /device:TPU:0, one launch (start us, length us, event | category | flops | bytes accessed | tf_op | source)
XLA Modules:
  0.0 106.2 jit_solution(3418234640794433520)
XLA Ops:
  0.6 99.0 %dilated_attention.1 = (bf16[128,4096]{1,0:T(8,128)(2,1)}, bf16[128,4096]{1,0:T(8,128)(2,1)}, bf16[128,4096]{1,0:T(8,128)(2,1)}, bf16[128,4096]{1,0:T(8,128)(2,1)}) custom-call(s32[2,8]{1,0:T(2,128)} %offsets.1, bf16[128,4096]{1,0:T(8,128)(2,1)} %query.1, bf16[128,4096]{1,0:T(8,128)(2,1)} %key.1, bf16[128,4096]{1,0:T(8,128)(2,1)} %value.1, ...), custom_call_target="tpu_custom_call" | custom-call | flops 4026531840 | bytes 8388608 | tf_op jit(solution)/shard_map/dilated_attention/pallas_call | solution.py:250
  99.6 0.0 copy-start.2
  99.6 2.4 %copy.13 = bf16[128,4096]{1,0:T(8,128)(2,1)} copy(bf16[128,4096]{1,0:T(8,128)(2,1)} %get-tuple-element.8) | data formatting | bytes 2097152
  102.0 0.0 copy-done.2
  102.0 0.0 copy-start.1
  102.0 1.0 copy.14
  103.0 0.6 copy-done.1
  103.6 0.0 copy-start
  103.6 1.0 copy.15
  104.6 0.6 copy-done
  105.2 1.0 copy.16
Async XLA Ops:
  99.6 2.4 %copy-start.2 = (bf16[128,4096]{1,0:T(8,128)(2,1)S(1)}, bf16[128,4096]{1,0:T(8,128)(2,1)}, u32[]{:S(2)}) copy-start(bf16[128,4096]{1,0:T(8,128)(2,1)} %get-tuple-element.9) | copy-start | bytes 3145732
  102.0 1.6 %copy-start.1 = (bf16[128,4096]{1,0:T(8,128)(2,1)S(1)}, bf16[128,4096]{1,0:T(8,128)(2,1)}, u32[]{:S(2)}) copy-start(bf16[128,4096]{1,0:T(8,128)(2,1)} %get-tuple-element.10) | copy-start | bytes 3145732
  103.6 1.6 %copy-start = (bf16[128,4096]{1,0:T(8,128)(2,1)S(1)}, bf16[128,4096]{1,0:T(8,128)(2,1)}, u32[]{:S(2)}) copy-start(bf16[128,4096]{1,0:T(8,128)(2,1)} %get-tuple-element.11) | copy-start | bytes 3145732

commit v2 on v1

--- a/solution.py
+++ b/solution.py
@@ -12,6 +12,7 @@
 UPPER_DILATION = 64
 MIDDLE_SEGMENTS = 4
 LOWEST = -1e30
+HELD_BACK = 3
 MESH = pl.DeviceIdType.MESH
 F32 = jnp.float32
 BF16 = jnp.bfloat16
@@ -54,6 +55,7 @@
     sources = (query, key, value, out_grad)
     results = (attended_out, query_out, key_out, value_out)
     scale = width ** -0.5
+    held = max(heads - HELD_BACK, 1)
 
     barrier = pltpu.get_barrier_semaphore()
     for step in range(1, group):
@@ -131,6 +133,11 @@
                     src, dst, out_send.at[a], out_recv.at[a],
                     device_id={"head": device}, device_id_type=MESH,
                 ).start()
+
+    def send_unless_held(head, a):
+        @pl.when(head >= held)
+        def _():
+            send_out(head, a)
 
     def attend(head):
         wait_for(mid_rows_in.at[head, pl.ds(0, mid_count - 1)], mid_recv.at[head])
@@ -166,9 +173,9 @@
         prob = weight * inverse
         dscore = (prob * (contract(v, do, 1, 1) - delta)).astype(BF16)
         staged[head, 0] = attended.T.astype(BF16)
-        send_out(head, 0)
+        send_unless_held(head, 0)
         staged[head, 1] = (contract(k, dscore, 0, 0) * scale).T.astype(BF16)
-        send_out(head, 1)
+        send_unless_held(head, 1)
         dk = contract(dscore, q, 1, 0) * scale
         dv = contract(prob.astype(BF16), do, 1, 0)
         partial[head % 2, 0] = dk[:tok]
@@ -203,9 +210,14 @@
         place = one_hot((tok, 2 * (mid_n + top_n)), 1, tok, offsets[0, head], offsets[1, head], 2)
         added = contract(place, both, 1, 0)
         staged[head, 2] = (partial[head % 2, 0] + added[:, :width]).astype(BF16)
-        send_out(head, 2)
+        send_unless_held(head, 2)
         staged[head, 3] = (partial[head % 2, 1] + added[:, width:]).astype(BF16)
-        send_out(head, 3)
+        send_unless_held(head, 3)
+
+    def release(head, carry):
+        for a in range(4):
+            send_out(head, a)
+        return carry
 
     gather_rows(0)
 
@@ -219,6 +231,10 @@
         @pl.when(head > 0)
         def _():
             finish(head - 1)
+
+        @pl.when(head == held)
+        def _():
+            lax.fori_loop(0, held, release, 0)
 
         return carry
 
@@ -234,6 +250,15 @@
     wait_for(top_rows_in.at[:, pl.ds(0, ctx_count - 1)], top_send)
     wait_for(mid_back_in.at[:, pl.ds(0, mid_count - 1)], mid_back_send)
     wait_for(top_back_in.at[:, pl.ds(0, ctx_count - 1)], top_back_send)
+
+
+def hand_over(*refs):
+    sources, results, sem = refs[:4], refs[4:8], refs[8]
+    copies = [pltpu.make_async_copy(src, dst, sem.at[i]) for i, (src, dst) in enumerate(zip(sources, results))]
+    for copy in copies:
+        copy.start()
+    for copy in copies:
+        copy.wait()
 
 
 def local(query, key, value, out_grad, offsets):
@@ -247,9 +272,9 @@
     dims = (ctx_count, mid_count, group, heads, own_rows, width)
     anywhere = pl.BlockSpec(memory_space=pl.ANY)
     dma = pltpu.SemaphoreType.DMA
-    return pl.pallas_call(
+    landed = pl.pallas_call(
         functools.partial(kernel, dims),
-        out_shape=tuple(jax.ShapeDtypeStruct(query.shape, BF16) for _ in range(4)),
+        out_shape=tuple(pltpu.VMEM(query.shape, BF16) for _ in range(4)),
         in_specs=[pl.BlockSpec(memory_space=pltpu.SMEM)] + [anywhere] * 4,
         out_specs=(anywhere,) * 4,
         scratch_shapes=[
@@ -277,6 +302,14 @@
         ),
         name="dilated_attention",
     )(offsets, query, key, value, out_grad)
+    return pl.pallas_call(
+        hand_over,
+        out_shape=tuple(jax.ShapeDtypeStruct(query.shape, BF16) for _ in range(4)),
+        in_specs=[anywhere] * 4,
+        out_specs=(anywhere,) * 4,
+        scratch_shapes=[dma((4,))],
+        name="hand_over",
+    )(*landed)
 
 
 def solution(mesh):

time: 106 us -> 232 us (2.19)
  Pallas kernels: 99 us -> 227 us
  local copies, waits for them, and re-layouts: 6.55 us -> 3.94 us
    pallas_call x1 -> x2, Pallas kernels: 99 us -> 227 us  [the longest x1 128 us: local(): pl.pallas_call(hand_over, out_shape=tuple((jax.ShapeDtypeStruct(query.sha...]
    unnamed x10 -> x8, local copies, waits for them, and re-layouts: 6.55 us -> 3.94 us
where the time goes in v2:
time: 232 us
  Pallas kernels  227 us (98%)
  local copies, waits for them, and re-layouts  3.94 us (2%)
    pallas_call x1, Pallas kernels, local(): pl.pallas_call(hand_over, out_shape=tuple((jax.ShapeDtypeStruct(query.sha...  128 us
    pallas_call x1, Pallas kernels, local(): pl.pallas_call(functools.partial(kernel, dims), out_shape=tuple((pltpu.VM...  98.9 us

profile of v2, /device:TPU:0, one launch (start us, length us, event | category | flops | bytes accessed | tf_op | source)
XLA Modules:
  0.0 231.7 jit_solution(13052419207224769601)
XLA Ops:
  0.6 98.9 %dilated_attention.1 = (bf16[128,4096]{1,0:T(8,128)(2,1)S(1)}, bf16[128,4096]{1,0:T(8,128)(2,1)S(1)}, bf16[128,4096]{1,0:T(8,128)(2,1)S(1)}, bf16[128,4096]{1,0:T(8,128)(2,1)S(1)}) custom-call(s32[2,8]{1,0:T(2,128)} %offsets.1, bf16[128,4096]{1,0:T(8,128)(2,1)} %query.1, bf16[128,4096]{1,0:T(8,128)(2,1)} %key.1, bf16[128,4096]{1,0:T(8,128)(2,1)} %value.1, ...), custom_call_target="tpu_custom_call" | custom-call | flops 4026531840 | bytes 8388608 | tf_op jit(solution)/shard_map/dilated_attention/pallas_call | solution.py:275
  99.5 0.0 copy-start
  99.5 1.0 copy-done
  100.5 0.0 copy-start.1
  100.5 1.0 copy-done.1
  101.5 0.0 copy-start.2
  101.5 1.0 copy-done.2
  102.5 0.0 copy-start.3
  102.5 1.0 copy-done.3
  103.5 128.2 %hand_over.1 = (bf16[128,4096]{1,0:T(8,128)(2,1)}, bf16[128,4096]{1,0:T(8,128)(2,1)}, bf16[128,4096]{1,0:T(8,128)(2,1)}, bf16[128,4096]{1,0:T(8,128)(2,1)}) custom-call(bf16[128,4096]{1,0:T(8,128)(2,1)} %copy-done, bf16[128,4096]{1,0:T(8,128)(2,1)} %copy-done.1, bf16[128,4096]{1,0:T(8,128)(2,1)} %copy-done.2, bf16[128,4096]{1,0:T(8,128)(2,1)} %copy-done.3), custom_call_target="tpu_custom_call" | custom-call | tf_op jit(solution)/shard_map/hand_over/pallas_call | solution.py:305
Async XLA Ops:
  99.5 1.0 copy-start
  100.5 1.0 copy-start.1
  101.5 1.0 copy-start.2
  102.5 1.0 copy-start.3

commit v3 on v1

--- a/solution.py
+++ b/solution.py
@@ -43,7 +43,7 @@
     mid_own, mid_rows_in, top_own, top_rows_in,
     mid_back, mid_back_in, top_back, top_back_in,
     in_recv, mid_recv, top_recv, mid_back_recv, top_back_recv, out_recv,
-    in_send, mid_send, top_send, mid_back_send, top_back_send, out_send,
+    in_send, mid_send, top_send, mid_back_send, top_back_send, out_send, entered,
 ):
     ctx_count, mid_count, group, heads, own_rows, width = dims
     tok = own_rows * group
@@ -55,16 +55,18 @@
     results = (attended_out, query_out, key_out, value_out)
     scale = width ** -0.5
 
+    def signal_ctx(sem, low, high):
+        def body(other, carry):
+            pl.semaphore_signal(sem, inc=1, device_id={"ctx": other}, device_id_type=MESH)
+            return carry
+
+        lax.fori_loop(low, high, body, 0)
+
     barrier = pltpu.get_barrier_semaphore()
     for step in range(1, group):
         pl.semaphore_signal(barrier, inc=1, device_id={"head": (me + step) % group}, device_id_type=MESH)
-
-    def greet(step, carry):
-        pl.semaphore_signal(barrier, inc=1, device_id={"ctx": (ctx + step) % ctx_count}, device_id_type=MESH)
-        return carry
-
-    lax.fori_loop(1, ctx_count, greet, 0)
-    pl.semaphore_wait(barrier, group - 1 + ctx_count - 1)
+    signal_ctx(barrier, ctx + 1, ctx_count)
+    pl.semaphore_wait(barrier, group - 1 + ctx)
 
     def columns(device, head):
         return pl.ds(pl.multiple_of((device * heads + head) * width, width), width)
@@ -88,6 +90,11 @@
         return carry
 
     lax.fori_loop(0, heads, send_in, 0)
+    signal_ctx(entered, 0, ctx)
+
+    @pl.when(ctx < ctx_count - 1)
+    def _():
+        pl.semaphore_wait(entered, ctx_count - 1 - ctx)
 
     def ring(count, place, base, src_of, dst, send_sem, recv_sem):
         def body(step, carry):
@@ -236,6 +243,15 @@
     wait_for(top_back_in.at[:, pl.ds(0, ctx_count - 1)], top_back_send)
 
 
+def hand_over(*refs):
+    sources, results, sem = refs[:4], refs[4:8], refs[8]
+    copies = [pltpu.make_async_copy(src, dst, sem.at[i]) for i, (src, dst) in enumerate(zip(sources, results))]
+    for copy in copies:
+        copy.start()
+    for copy in copies:
+        copy.wait()
+
+
 def local(query, key, value, out_grad, offsets):
     ctx_count, group = lax.axis_size("ctx"), lax.axis_size("head")
     heads = offsets.shape[1]
@@ -247,9 +263,9 @@
     dims = (ctx_count, mid_count, group, heads, own_rows, width)
     anywhere = pl.BlockSpec(memory_space=pl.ANY)
     dma = pltpu.SemaphoreType.DMA
-    return pl.pallas_call(
+    landed = pl.pallas_call(
         functools.partial(kernel, dims),
-        out_shape=tuple(jax.ShapeDtypeStruct(query.shape, BF16) for _ in range(4)),
+        out_shape=tuple(pltpu.VMEM(query.shape, BF16) for _ in range(4)),
         in_specs=[pl.BlockSpec(memory_space=pltpu.SMEM)] + [anywhere] * 4,
         out_specs=(anywhere,) * 4,
         scratch_shapes=[
@@ -265,10 +281,10 @@
             pltpu.VMEM((heads, ctx_count, 2 * top_n, width), BF16),
             pltpu.VMEM((heads, ctx_count, 2 * top_n, width), BF16),
             dma((heads,)), dma((heads,)), dma((heads,)), dma((heads,)), dma((heads,)), dma((4,)),
-            dma((4,)), dma, dma, dma, dma, dma((4,)),
+            dma((4,)), dma, dma, dma, dma, dma((4,)), pltpu.SemaphoreType.REGULAR,
         ],
         compiler_params=pltpu.CompilerParams(
-            collective_id=0, has_side_effects=True, vmem_limit_bytes=56 * 1024 * 1024
+            collective_id=0, has_side_effects=True, vmem_limit_bytes=59 * 1024 * 1024
         ),
         cost_estimate=pl.CostEstimate(
             flops=12 * heads * tok * (tok + 128) * width,
@@ -277,6 +293,15 @@
         ),
         name="dilated_attention",
     )(offsets, query, key, value, out_grad)
+    return pl.pallas_call(
+        hand_over,
+        out_shape=tuple(jax.ShapeDtypeStruct(query.shape, BF16) for _ in range(4)),
+        in_specs=[anywhere] * 4,
+        out_specs=(anywhere,) * 4,
+        scratch_shapes=[dma((4,))],
+        compiler_params=pltpu.CompilerParams(vmem_limit_bytes=16 * 1024 * 1024),
+        name="hand_over",
+    )(*(pltpu.with_memory_space_constraint(x, pltpu.VMEM) for x in landed))
 
 
 def solution(mesh):

time: 106 us -> 98.1 us (0.925)
  local copies, waits for them, and re-layouts: 6.55 us -> 0 us
  Pallas kernels: 99 us -> 97.3 us
    unnamed x10 -> x0, local copies, waits for them, and re-layouts: 6.55 us -> none
    pallas_call x1 -> x2, Pallas kernels: 99 us -> 97.3 us  [the longest x1 95.2 us: local(): pl.pallas_call(functools.partial(kernel, dims), out_shape=tuple((pltpu.VM...]
where the time goes in v3:
time: 98.1 us; the launch traced here: 97.9 us
  Pallas kernels  97.3 us (99%)
    pallas_call x1, Pallas kernels, local(): pl.pallas_call(functools.partial(kernel, dims), out_shape=tuple((pltpu.VM...  95.2 us
    pallas_call x1, Pallas kernels, local(): pl.pallas_call(hand_over, out_shape=tuple((jax.ShapeDtypeStruct(query.sha...  2.04 us

profile of v3, /device:TPU:0, one launch (start us, length us, event | category | flops | bytes accessed | tf_op | source)
XLA Modules:
  0.0 97.9 jit_solution(90232233975061994)
XLA Ops:
  0.6 95.2 %dilated_attention.1 = (bf16[128,4096]{1,0:T(8,128)(2,1)S(1)}, bf16[128,4096]{1,0:T(8,128)(2,1)S(1)}, bf16[128,4096]{1,0:T(8,128)(2,1)S(1)}, bf16[128,4096]{1,0:T(8,128)(2,1)S(1)}) custom-call(s32[2,8]{1,0:T(2,128)} %offsets.1, bf16[128,4096]{1,0:T(8,128)(2,1)} %query.1, bf16[128,4096]{1,0:T(8,128)(2,1)} %key.1, bf16[128,4096]{1,0:T(8,128)(2,1)} %value.1, ...), custom_call_target="tpu_custom_call" | custom-call | flops 4026531840 | bytes 8388608 | tf_op jit(solution)/shard_map/dilated_attention/pallas_call | solution.py:266
  95.9 2.0 %hand_over.1 = (bf16[128,4096]{1,0:T(8,128)(2,1)}, bf16[128,4096]{1,0:T(8,128)(2,1)}, bf16[128,4096]{1,0:T(8,128)(2,1)}, bf16[128,4096]{1,0:T(8,128)(2,1)}) custom-call(bf16[128,4096]{1,0:T(8,128)(2,1)S(1)} %get-tuple-element.8.refs_0_, bf16[128,4096]{1,0:T(8,128)(2,1)S(1)} %get-tuple-element.9.refs_1_, bf16[128,4096]{1,0:T(8,128)(2,1)S(1)} %get-tuple-element.10.refs_2_, ...), custom_call_target="tpu_custom_call" | custom-call | tf_op jit(solution)/shard_map/hand_over/pallas_call | solution.py:296

commit v4 on v3

--- a/solution.py
+++ b/solution.py
@@ -12,6 +12,7 @@
 UPPER_DILATION = 64
 MIDDLE_SEGMENTS = 4
 LOWEST = -1e30
+BUNDLE = 2
 MESH = pl.DeviceIdType.MESH
 F32 = jnp.float32
 BF16 = jnp.bfloat16
@@ -68,28 +69,33 @@
     signal_ctx(barrier, ctx + 1, ctx_count)
     pl.semaphore_wait(barrier, group - 1 + ctx)
 
-    def columns(device, head):
-        return pl.ds(pl.multiple_of((device * heads + head) * width, width), width)
+    wide = BUNDLE * width
+
+    def columns(device, bundle):
+        return pl.ds(pl.multiple_of(device * heads * width + bundle * wide, wide), wide)
+
+    def lanes(head):
+        return pl.ds(pl.multiple_of(head % BUNDLE * width, width), width)
 
     def rows_of(device):
         return pl.ds(pl.multiple_of(device * own_rows, own_rows), own_rows)
 
-    def send_in(head, carry):
+    def send_in(bundle, carry):
         for step in range(group):
             device = (me + step) % group
             for a in (1, 2, 0, 3):
-                src = sources[a].at[:, columns(device, head)]
-                dst = arrived.at[head, a, rows_of(me)]
+                src = sources[a].at[:, columns(device, bundle)]
+                dst = arrived.at[bundle, a, rows_of(me)]
                 if step == 0:
-                    pltpu.make_async_copy(src, dst, in_recv.at[head]).start()
+                    pltpu.make_async_copy(src, dst, in_recv.at[bundle]).start()
                 else:
                     pltpu.make_async_remote_copy(
-                        src, dst, in_send.at[a], in_recv.at[head],
+                        src, dst, in_send.at[a], in_recv.at[bundle],
                         device_id={"head": device}, device_id_type=MESH,
                     ).start()
         return carry
 
-    lax.fori_loop(0, heads, send_in, 0)
+    lax.fori_loop(0, heads // BUNDLE, send_in, 0)
     signal_ctx(entered, 0, ctx)
 
     @pl.when(ctx < ctx_count - 1)
@@ -111,10 +117,15 @@
         pltpu.make_async_copy(ref, ref, sem).wait()
 
     def gather_rows(head):
-        wait_for(arrived.at[head], in_recv.at[head])
+        bundle = head // BUNDLE
+
+        @pl.when(head % BUNDLE == 0)
+        def _():
+            wait_for(arrived.at[bundle], in_recv.at[bundle])
+
         pick = one_hot((mid_n + top_n, tok), 0, tok, offsets[0, head], offsets[1, head], 1)
-        key_rows = contract(pick, arrived[head, 1], 1, 0)
-        value_rows = contract(pick, arrived[head, 2], 1, 0)
+        key_rows = contract(pick, arrived[bundle, 1, :, lanes(head)], 1, 0)
+        value_rows = contract(pick, arrived[bundle, 2, :, lanes(head)], 1, 0)
         mid = jnp.concatenate([key_rows[:mid_n], value_rows[:mid_n]], 0).astype(BF16)
         top = jnp.concatenate([key_rows[mid_n:], value_rows[mid_n:]], 0).astype(BF16)
         mid_own[head] = mid
@@ -126,18 +137,23 @@
         ring(mid_count, mid_me, mid_base, lambda other: mid_own.at[head], mid_rows_in.at[head, mid_me],
              mid_send, mid_recv.at[head])
 
-    def send_out(head, a):
-        for step in range(group):
-            device = (me + step) % group
-            src = staged.at[head, a, rows_of(device)]
-            dst = results[a].at[:, columns(me, head)]
-            if step == 0:
-                pltpu.make_async_copy(src, dst, out_recv.at[a]).start()
-            else:
-                pltpu.make_async_remote_copy(
-                    src, dst, out_send.at[a], out_recv.at[a],
-                    device_id={"head": device}, device_id_type=MESH,
-                ).start()
+    def hand_in(head, a, rows):
+        bundle = head // BUNDLE
+        staged[bundle, a, :, lanes(head)] = rows.astype(BF16)
+
+        @pl.when(head % BUNDLE == BUNDLE - 1)
+        def _():
+            for step in range(group):
+                device = (me + step) % group
+                src = staged.at[bundle, a, rows_of(device)]
+                dst = results[a].at[:, columns(me, bundle)]
+                if step == 0:
+                    pltpu.make_async_copy(src, dst, out_recv.at[a]).start()
+                else:
+                    pltpu.make_async_remote_copy(
+                        src, dst, out_send.at[a], out_recv.at[a],
+                        device_id={"head": device}, device_id_type=MESH,
+                    ).start()
 
     def attend(head):
         wait_for(mid_rows_in.at[head, pl.ds(0, mid_count - 1)], mid_recv.at[head])
@@ -145,14 +161,15 @@
         mid_in = mid_rows_in[head].astype(F32)
         top_in = top_rows_in[head].astype(F32)
         mid_all, top_all = mid_count * mid_n, ctx_count * top_n
-        q, do = arrived[head, 0], arrived[head, 3]
+        bundle = head // BUNDLE
+        q, do = arrived[bundle, 0, :, lanes(head)], arrived[bundle, 3, :, lanes(head)]
         k = jnp.concatenate([
-            arrived[head, 1],
+            arrived[bundle, 1, :, lanes(head)],
             mid_in[:, :mid_n].reshape(mid_all, width).astype(BF16),
             top_in[:, :top_n].reshape(top_all, width).astype(BF16),
         ], 0)
         v = jnp.concatenate([
-            arrived[head, 2],
+            arrived[bundle, 2, :, lanes(head)],
             mid_in[:, mid_n:].reshape(mid_all, width).astype(BF16),
             top_in[:, top_n:].reshape(top_all, width).astype(BF16),
         ], 0)
@@ -172,10 +189,8 @@
         delta = jnp.sum(do.astype(F32).T * attended, 0, keepdims=True)
         prob = weight * inverse
         dscore = (prob * (contract(v, do, 1, 1) - delta)).astype(BF16)
-        staged[head, 0] = attended.T.astype(BF16)
-        send_out(head, 0)
-        staged[head, 1] = (contract(k, dscore, 0, 0) * scale).T.astype(BF16)
-        send_out(head, 1)
+        hand_in(head, 0, attended.T)
+        hand_in(head, 1, (contract(k, dscore, 0, 0) * scale).T)
         dk = contract(dscore, q, 1, 0) * scale
         dv = contract(prob.astype(BF16), do, 1, 0)
         partial[head % 2, 0] = dk[:tok]
@@ -209,10 +224,8 @@
         both = jnp.concatenate([high, rows - high], 0).astype(BF16)
         place = one_hot((tok, 2 * (mid_n + top_n)), 1, tok, offsets[0, head], offsets[1, head], 2)
         added = contract(place, both, 1, 0)
-        staged[head, 2] = (partial[head % 2, 0] + added[:, :width]).astype(BF16)
-        send_out(head, 2)
-        staged[head, 3] = (partial[head % 2, 1] + added[:, width:]).astype(BF16)
-        send_out(head, 3)
+        hand_in(head, 2, partial[head % 2, 0] + added[:, :width])
+        hand_in(head, 3, partial[head % 2, 1] + added[:, width:])
 
     gather_rows(0)
 
@@ -269,8 +282,8 @@
         in_specs=[pl.BlockSpec(memory_space=pltpu.SMEM)] + [anywhere] * 4,
         out_specs=(anywhere,) * 4,
         scratch_shapes=[
-            pltpu.VMEM((heads, 4, tok, width), BF16),
-            pltpu.VMEM((heads, 4, tok, width), BF16),
+            pltpu.VMEM((heads // BUNDLE, 4, tok, BUNDLE * width), BF16),
+            pltpu.VMEM((heads // BUNDLE, 4, tok, BUNDLE * width), BF16),
             pltpu.VMEM((2, 2, tok, width), F32),
             pltpu.VMEM((heads, 2 * mid_n, width), BF16),
             pltpu.VMEM((heads, mid_count, 2 * mid_n, width), BF16),

time: 98.1 us -> 97.8 us (level)
  no operation moved by 1% of the time
where the time goes in v4:
time: 97.8 us; the launch traced here: 97.5 us
  Pallas kernels  96.9 us (99%)
    pallas_call x1, Pallas kernels, local(): pl.pallas_call(functools.partial(kernel, dims), out_shape=tuple((pltpu.VM...  94.8 us
    pallas_call x1, Pallas kernels, local(): pl.pallas_call(hand_over, out_shape=tuple((jax.ShapeDtypeStruct(query.sha...  2.04 us

profile of v4, /device:TPU:0, one launch (start us, length us, event | category | flops | bytes accessed | tf_op | source)
XLA Modules:
  0.0 97.5 jit_solution(17195439207218271631)
XLA Ops:
  0.6 94.8 %dilated_attention.1 = (bf16[128,4096]{1,0:T(8,128)(2,1)S(1)}, bf16[128,4096]{1,0:T(8,128)(2,1)S(1)}, bf16[128,4096]{1,0:T(8,128)(2,1)S(1)}, bf16[128,4096]{1,0:T(8,128)(2,1)S(1)}) custom-call(s32[2,8]{1,0:T(2,128)} %offsets.1, bf16[128,4096]{1,0:T(8,128)(2,1)} %query.1, bf16[128,4096]{1,0:T(8,128)(2,1)} %key.1, bf16[128,4096]{1,0:T(8,128)(2,1)} %value.1, ...), custom_call_target="tpu_custom_call" | custom-call | flops 4026531840 | bytes 8388608 | tf_op jit(solution)/shard_map/dilated_attention/pallas_call | solution.py:279
  95.5 2.0 %hand_over.1 = (bf16[128,4096]{1,0:T(8,128)(2,1)}, bf16[128,4096]{1,0:T(8,128)(2,1)}, bf16[128,4096]{1,0:T(8,128)(2,1)}, bf16[128,4096]{1,0:T(8,128)(2,1)}) custom-call(bf16[128,4096]{1,0:T(8,128)(2,1)S(1)} %get-tuple-element.8.refs_0_, bf16[128,4096]{1,0:T(8,128)(2,1)S(1)} %get-tuple-element.9.refs_1_, bf16[128,4096]{1,0:T(8,128)(2,1)S(1)} %get-tuple-element.10.refs_2_, ...), custom_call_target="tpu_custom_call" | custom-call | tf_op jit(solution)/shard_map/hand_over/pallas_call | solution.py:309

commit v5 on v4

--- a/solution.py
+++ b/solution.py
@@ -13,6 +13,8 @@
 MIDDLE_SEGMENTS = 4
 LOWEST = -1e30
 BUNDLE = 2
+CORES = 2
+HAND_OVER_CUTS = 4
 MESH = pl.DeviceIdType.MESH
 F32 = jnp.float32
 BF16 = jnp.bfloat16
@@ -55,6 +57,11 @@
     sources = (query, key, value, out_grad)
     results = (attended_out, query_out, key_out, value_out)
     scale = width ** -0.5
+    chips = group // CORES
+    partners = [
+        (me // CORES + chip) % chips * CORES + (me + core) % CORES
+        for chip in range(1, chips) for core in range(CORES)
+    ] + [me // CORES * CORES + (me + core) % CORES for core in range(1, CORES)] + [me]
 
     def signal_ctx(sem, low, high):
         def body(other, carry):
@@ -81,12 +88,11 @@
         return pl.ds(pl.multiple_of(device * own_rows, own_rows), own_rows)
 
     def send_in(bundle, carry):
-        for step in range(group):
-            device = (me + step) % group
+        for device in partners:
             for a in (1, 2, 0, 3):
                 src = sources[a].at[:, columns(device, bundle)]
                 dst = arrived.at[bundle, a, rows_of(me)]
-                if step == 0:
+                if device is me:
                     pltpu.make_async_copy(src, dst, in_recv.at[bundle]).start()
                 else:
                     pltpu.make_async_remote_copy(
@@ -143,11 +149,10 @@
 
         @pl.when(head % BUNDLE == BUNDLE - 1)
         def _():
-            for step in range(group):
-                device = (me + step) % group
+            for device in partners:
                 src = staged.at[bundle, a, rows_of(device)]
                 dst = results[a].at[:, columns(me, bundle)]
-                if step == 0:
+                if device is me:
                     pltpu.make_async_copy(src, dst, out_recv.at[a]).start()
                 else:
                     pltpu.make_async_remote_copy(
@@ -227,23 +232,22 @@
         hand_in(head, 2, partial[head % 2, 0] + added[:, :width])
         hand_in(head, 3, partial[head % 2, 1] + added[:, width:])
 
-    gather_rows(0)
-
     def turn(head, carry):
-        @pl.when(head < heads - 1)
-        def _():
-            gather_rows(head + 1)
-
-        attend(head)
-
-        @pl.when(head > 0)
-        def _():
-            finish(head - 1)
+        @pl.when(head < heads)
+        def _():
+            gather_rows(head)
+
+        @pl.when((head >= 1) & (head <= heads))
+        def _():
+            attend(head - 1)
+
+        @pl.when(head >= 2)
+        def _():
+            finish(head - 2)
 
         return carry
 
-    lax.fori_loop(0, heads, turn, 0)
-    finish(heads - 1)
+    lax.fori_loop(0, heads + 2, turn, 0)
 
     others = pl.ds(0, own_rows * (group - 1))
     for a in range(4):
@@ -257,8 +261,12 @@
 
 
 def hand_over(*refs):
-    sources, results, sem = refs[:4], refs[4:8], refs[8]
-    copies = [pltpu.make_async_copy(src, dst, sem.at[i]) for i, (src, dst) in enumerate(zip(sources, results))]
+    sources, results, sems = refs[:4], refs[4:8], refs[8]
+    rows = sources[0].shape[0] // HAND_OVER_CUTS
+    copies = [
+        pltpu.make_async_copy(src.at[pl.ds(cut * rows, rows)], dst.at[pl.ds(cut * rows, rows)], sems.at[i, cut])
+        for i, (src, dst) in enumerate(zip(sources, results)) for cut in range(HAND_OVER_CUTS)
+    ]
     for copy in copies:
         copy.start()
     for copy in copies:
@@ -311,7 +319,7 @@
         out_shape=tuple(jax.ShapeDtypeStruct(query.shape, BF16) for _ in range(4)),
         in_specs=[anywhere] * 4,
         out_specs=(anywhere,) * 4,
-        scratch_shapes=[dma((4,))],
+        scratch_shapes=[dma((4, HAND_OVER_CUTS))],
         compiler_params=pltpu.CompilerParams(vmem_limit_bytes=16 * 1024 * 1024),
         name="hand_over",
     )(*(pltpu.with_memory_space_constraint(x, pltpu.VMEM) for x in landed))

time: 97.8 us -> 98.3 us (level)
  no operation moved by 1% of the time
where the time goes in v5:
time: 98.3 us; the launch traced here: 98.1 us
  Pallas kernels  97.5 us (99%)
    pallas_call x1, Pallas kernels, local(): pl.pallas_call(functools.partial(kernel, dims), out_shape=tuple((pltpu.VM...  95.3 us
    pallas_call x1, Pallas kernels, local(): pl.pallas_call(hand_over, out_shape=tuple((jax.ShapeDtypeStruct(query.sha...  2.14 us

profile of v5, /device:TPU:0, one launch (start us, length us, event | category | flops | bytes accessed | tf_op | source)
XLA Modules:
  0.0 98.1 jit_solution(10712376833187513516)
XLA Ops:
  0.6 95.3 %dilated_attention.1 = (bf16[128,4096]{1,0:T(8,128)(2,1)S(1)}, bf16[128,4096]{1,0:T(8,128)(2,1)S(1)}, bf16[128,4096]{1,0:T(8,128)(2,1)S(1)}, bf16[128,4096]{1,0:T(8,128)(2,1)S(1)}) custom-call(s32[2,8]{1,0:T(2,128)} %offsets.1, bf16[128,4096]{1,0:T(8,128)(2,1)} %query.1, bf16[128,4096]{1,0:T(8,128)(2,1)} %key.1, bf16[128,4096]{1,0:T(8,128)(2,1)} %value.1, ...), custom_call_target="tpu_custom_call" | custom-call | flops 4026531840 | bytes 8388608 | tf_op jit(solution)/shard_map/dilated_attention/pallas_call | solution.py:287
  96.0 2.1 %hand_over.1 = (bf16[128,4096]{1,0:T(8,128)(2,1)}, bf16[128,4096]{1,0:T(8,128)(2,1)}, bf16[128,4096]{1,0:T(8,128)(2,1)}, bf16[128,4096]{1,0:T(8,128)(2,1)}) custom-call(bf16[128,4096]{1,0:T(8,128)(2,1)S(1)} %get-tuple-element.8.refs_0_, bf16[128,4096]{1,0:T(8,128)(2,1)S(1)} %get-tuple-element.9.refs_1_, bf16[128,4096]{1,0:T(8,128)(2,1)S(1)} %get-tuple-element.10.refs_2_, ...), custom_call_target="tpu_custom_call" | custom-call | tf_op jit(solution)/shard_map/hand_over/pallas_call | solution.py:317

commit v6 on v5

--- a/solution.py
+++ b/solution.py
@@ -14,7 +14,7 @@
 LOWEST = -1e30
 BUNDLE = 2
 CORES = 2
-HAND_OVER_CUTS = 4
+HAND_OVER_CUTS = 2
 MESH = pl.DeviceIdType.MESH
 F32 = jnp.float32
 BF16 = jnp.bfloat16
@@ -232,22 +232,23 @@
         hand_in(head, 2, partial[head % 2, 0] + added[:, :width])
         hand_in(head, 3, partial[head % 2, 1] + added[:, width:])
 
+    gather_rows(0)
+
     def turn(head, carry):
-        @pl.when(head < heads)
+        @pl.when(head < heads - 1)
         def _():
-            gather_rows(head)
-
-        @pl.when((head >= 1) & (head <= heads))
+            gather_rows(head + 1)
+
+        attend(head)
+
+        @pl.when(head > 0)
         def _():
-            attend(head - 1)
-
-        @pl.when(head >= 2)
-        def _():
-            finish(head - 2)
+            finish(head - 1)
 
         return carry
 
-    lax.fori_loop(0, heads + 2, turn, 0)
+    lax.fori_loop(0, heads, turn, 0)
+    finish(heads - 1)
 
     others = pl.ds(0, own_rows * (group - 1))
     for a in range(4):
@@ -267,8 +268,8 @@
         pltpu.make_async_copy(src.at[pl.ds(cut * rows, rows)], dst.at[pl.ds(cut * rows, rows)], sems.at[i, cut])
         for i, (src, dst) in enumerate(zip(sources, results)) for cut in range(HAND_OVER_CUTS)
     ]
-    for copy in copies:
-        copy.start()
+    for i, copy in enumerate(copies):
+        copy.start(priority=i % 2)
     for copy in copies:
         copy.wait()
 

time: 98.3 us -> 98.2 us (level)
  no operation moved by 1% of the time
where the time goes in v6:
time: 98.2 us; the launch traced here: 98.1 us
  Pallas kernels  97.4 us (99%)
    pallas_call x1, Pallas kernels, local(): pl.pallas_call(functools.partial(kernel, dims), out_shape=tuple((pltpu.VM...  95.3 us
    pallas_call x1, Pallas kernels, local(): pl.pallas_call(hand_over, out_shape=tuple((jax.ShapeDtypeStruct(query.sha...  2.07 us

profile of v6, /device:TPU:0, one launch (start us, length us, event | category | flops | bytes accessed | tf_op | source)
XLA Modules:
  0.0 98.1 jit_solution(6865026416683973697)
XLA Ops:
  0.6 95.3 %dilated_attention.1 = (bf16[128,4096]{1,0:T(8,128)(2,1)S(1)}, bf16[128,4096]{1,0:T(8,128)(2,1)S(1)}, bf16[128,4096]{1,0:T(8,128)(2,1)S(1)}, bf16[128,4096]{1,0:T(8,128)(2,1)S(1)}) custom-call(s32[2,8]{1,0:T(2,128)} %offsets.1, bf16[128,4096]{1,0:T(8,128)(2,1)} %query.1, bf16[128,4096]{1,0:T(8,128)(2,1)} %key.1, bf16[128,4096]{1,0:T(8,128)(2,1)} %value.1, ...), custom_call_target="tpu_custom_call" | custom-call | flops 4026531840 | bytes 8388608 | tf_op jit(solution)/shard_map/dilated_attention/pallas_call | solution.py:288
  96.0 2.1 %hand_over.1 = (bf16[128,4096]{1,0:T(8,128)(2,1)}, bf16[128,4096]{1,0:T(8,128)(2,1)}, bf16[128,4096]{1,0:T(8,128)(2,1)}, bf16[128,4096]{1,0:T(8,128)(2,1)}) custom-call(bf16[128,4096]{1,0:T(8,128)(2,1)S(1)} %get-tuple-element.8.refs_0_, bf16[128,4096]{1,0:T(8,128)(2,1)S(1)} %get-tuple-element.9.refs_1_, bf16[128,4096]{1,0:T(8,128)(2,1)S(1)} %get-tuple-element.10.refs_2_, ...), custom_call_target="tpu_custom_call" | custom-call | tf_op jit(solution)/shard_map/hand_over/pallas_call | solution.py:318
